TPU v7x, 128 devices: a whole 4x4x4 slice. The times are simulated.
128 devices in a mesh: wide: 16 (over z, x), narrow: 8 (over y, core).
Axes of the slice: x: 4, y: 4, z: 4, core: 2. Of those that a mesh axis runs over, the one named last changes fastest.
Arguments:
- density: bfloat16 [4, 4096, 4096], P(None, 'wide', 'narrow'), may hold values from -6 to 6
- coefficients: bfloat16 [1024, 256, 4096], P(('wide', 'narrow')), may hold values from -0.5 to 0.5
- task_blocks: int32 [1024, 2], P(('wide', 'narrow')), may hold values from 0 to 63, as said below
- task_live: int32 [128], P(('wide', 'narrow')), may hold values from 1 to 8, as said below
Outputs:
- exchange_matrix: float32 [4, 4096, 4096], P(None, 'wide', 'narrow')
Inputs may be any that keep to these rules, and one draw needn't show every extreme that they name: `task_blocks`: for the device i of the joint axis wide+narrow (i = w * 8 + n), every slot's first block r lies in the block column group of n: n * 8 <= r < (n + 1) * 8. The second blocks c of the 8 slots of one device lie in 8 different stripes c // 4. A pair may occur on several devices. The live tasks of a device are its first task_live slots; some device has all 8 live.
All inputs are finite; a program needn't handle non-finite values.
Results may differ from a plain program's by a relative error of at most 0.0028.
Values may be sent and summed in bfloat16 or wider, within the bound.
A program may use at most 192 MiB of HBM per device.

v0:
```python
import jax
import jax.numpy as jnp
from jax import lax
from jax.sharding import PartitionSpec as P

BF = 64


def block_term(coef_rows, dens_flat):
    aux_count = coef_rows.shape[0]
    dens_count = dens_flat.shape[0] // (BF * BF)
    coef_mat = coef_rows.reshape(aux_count, BF, BF)
    dens_mat = dens_flat.reshape(dens_count, BF, BF)
    halves = lax.dot_general(
        coef_mat, dens_mat, (((2,), (1,)), ((), ())), preferred_element_type=jnp.float32
    ).astype(jnp.bfloat16)
    result = lax.dot_general(
        halves, coef_mat, (((0, 3), (0, 1)), ((), ())), preferred_element_type=jnp.float32
    )
    return jnp.transpose(result, (1, 0, 2)).reshape(dens_count * BF * BF)


def run_slots(coef_stack, dens_stack, lower, upper, initial, displace):

    def step(position, running):
        local_pos = position - displace
        coef_rows = lax.dynamic_index_in_dim(coef_stack, local_pos, 0, keepdims=False)
        dens_flat = lax.dynamic_index_in_dim(dens_stack, local_pos, 0, keepdims=False)
        return lax.dynamic_update_index_in_dim(
            running, block_term(coef_rows, dens_flat), local_pos, 0
        )

    return lax.fori_loop(
        jnp.asarray(lower, jnp.int32), jnp.asarray(upper, jnp.int32), step, initial
    )


def pack_slots(keys, key_count, partials):
    slots_count = keys.shape[0]
    selector = keys[None, :] == jnp.arange(key_count, dtype=jnp.int32)[:, None]
    slot_task = jnp.sum(
        jnp.where(selector, jnp.arange(slots_count, dtype=jnp.int32)[None, :], 0), axis=1
    )
    filled = jnp.any(selector, axis=1)
    values = jnp.where(filled[:, None], partials[slot_task], 0.0)
    return (values, slot_task)


def local(density, coefficients, task_blocks, task_live):
    wide_count = lax.axis_size("wide")
    narrow_count = lax.axis_size("narrow")
    ratio = wide_count // narrow_count
    stripe = density.shape[1] // BF
    group = density.shape[2] // BF
    dens_count = density.shape[0]
    slots_count = coefficients.shape[0]
    flat_size = dens_count * BF * BF
    column = lax.axis_index("narrow")
    row_blk = task_blocks[:, 0]
    col_blk = task_blocks[:, 1]
    live_count = task_live[0]
    local_row = row_blk - column * group
    col_stripe = col_blk // stripe
    portion = lax.all_gather(density, "wide", axis=1, tiled=True)
    height = portion.shape[1]

    def single(previous, cblock, lrow):
        offset = cblock * BF
        inside = (offset >= 0) & (offset < height)
        corner_row = jnp.clip(offset, 0, height - BF)
        sliced = lax.dynamic_slice(
            portion, (jnp.zeros((), jnp.int32), corner_row, lrow * BF), (portion.shape[0], BF, BF)
        )
        return jnp.where(inside, sliced.reshape(-1), previous)

    blocks = jax.vmap(single)(jnp.zeros((slots_count, flat_size), jnp.bfloat16), col_blk, local_row)
    empty_terms = jnp.zeros((slots_count, flat_size), jnp.float32)
    partials = run_slots(coefficients, blocks, 0, live_count, empty_terms, 0)
    target_wide = row_blk // stripe
    target_narrow = col_blk // group
    bucket = col_stripe % ratio
    tile_code = row_blk % stripe * group + col_blk % group
    keys = target_narrow * ratio + bucket
    values, slot_task = pack_slots(keys, narrow_count * ratio, partials)
    values = values.reshape(narrow_count, ratio, flat_size)
    details = jnp.stack([target_wide % ratio, tile_code], axis=1)
    details_out = details[slot_task].reshape(narrow_count, ratio, 2)
    middle_values, middle_details = (
        lax.all_to_all(values, "narrow", split_axis=0, concat_axis=0, tiled=True),
        lax.all_to_all(details_out, "narrow", split_axis=0, concat_axis=0, tiled=True),
    )
    matching = middle_details[:, None, :, 0] == jnp.arange(ratio, dtype=jnp.int32)[None, :, None]
    forwarded = jnp.where(matching[..., None], middle_values[:, None, :, :], 0.0).reshape(
        wide_count, ratio, flat_size
    )
    forwarded_codes = jnp.broadcast_to(
        middle_details[:, None, :, 1], (narrow_count, ratio, ratio)
    ).reshape(wide_count, ratio)
    got_values, got_codes = (
        lax.all_to_all(forwarded, "wide", split_axis=0, concat_axis=0, tiled=True),
        lax.all_to_all(forwarded_codes, "wide", split_axis=0, concat_axis=0, tiled=True),
    )
    flat_values = got_values.reshape(-1, flat_size)
    flat_codes = got_codes.reshape(-1)
    tile = jnp.zeros((stripe * group, flat_size), jnp.float32).at[flat_codes].add(flat_values)
    tile = tile.reshape(stripe, group, dens_count, BF, BF).transpose(2, 0, 3, 1, 4)
    return tile.reshape(dens_count, stripe * BF, group * BF)


def solution(mesh):
    in_specs = (
        P(None, "wide", "narrow"),
        P(("wide", "narrow"), None, None),
        P(("wide", "narrow"), None),
        P(("wide", "narrow")),
    )
    out_specs = P(None, "wide", "narrow")
    return jax.shard_map(local, mesh=mesh, in_specs=in_specs, out_specs=out_specs, check_vma=False)
```

profile of v0, /device:TPU:0, one launch (start us, length us, event | category | flops | bytes accessed | tf_op | source)
XLA Modules:
  0.0 397.5 jit_solution(3174650851098416446)
XLA Ops:
  7.3 0.8 and_select_fusion.5
  10.2 0.7 copy.61
  10.9 4.6 %all-to-all-start = ((s32[8,2,2]{1,2,0:T(2,128)}), s32[8,2,2]{1,2,0:T(2,128)S(1)}, u32[]{:S(2)}, u32[]{:S(2)}) async-start(s32[8,2,2]{1,2,0:T(2,128)} %copy.61), calls=%async_computation | async-start | bytes 16384 | tf_op jit(solution)/shard_map/all_to_all | solution.py:90
  16.4 107.1 %all-gather.2.cloned.1.call-done = bf16[4,4096,512]{2,1,0:T(8,128)(2,1)} async-done(((bf16[4,256,512]{2,1,0:T(8,128)(2,1)}), bf16[4,4096,512]{2,1,0:T(8,128)(2,1)}) %all-gather.2.cloned.1.call-update) | async-done | bytes 16777232 | tf_op jit(solution)/shard_map/all_gather | solution.py:64
  123.4 23.2 %while.12 = (s32[]{:T(128)}, bf16[4,4096,512]{2,1,0:T(8,128)(2,1)}, s32[8,3]{0,1:T(4,128)S(1)}, bf16[8,4,64,64]{3,2,1,0:T(8,128)(2,1)S(1)}, s32[]{:T(128)}) while((s32[]{:T(128)}, bf16[4,4096,512]{2,1,0:T(8,128)(2,1)}, s32[8,3]{0,1:T(4,128)S(1)}, bf16[8,4,64,64]{3,2,1,0:T(8,128)(2,1)S(1)}, s32[]{:T(128)}) %tuple.46), condition=%wide.while_cond, body=%wide.while_body.sunk | while | flops 2 | bytes 98421 | solution.py:71
  124.1 2.3 bitcast_dynamic-update-slice_fusion.2
  127.0 2.3 bitcast_dynamic-update-slice_fusion.2
  129.9 2.3 bitcast_dynamic-update-slice_fusion.2
  132.8 2.3 bitcast_dynamic-update-slice_fusion.2
  135.7 2.3 bitcast_dynamic-update-slice_fusion.2
  138.6 2.3 bitcast_dynamic-update-slice_fusion.2
  141.5 2.3 bitcast_dynamic-update-slice_fusion.2
  144.4 2.3 bitcast_dynamic-update-slice_fusion.2
  147.2 20.1 %while.11 = (s32[]{:T(128)}, f32[8,16384]{1,0:T(8,128)S(1)}, s32[]{:T(128)}, bf16[8,256,4096]{2,1,0:T(8,128)(2,1)}, bf16[8,16384]{1,0:T(8,128)(2,1)S(1)}, /*index=5*/s32[]{:T(128)}, s32[]{:T(128)}, s32[]{:T(128)}) while((s32[]{:T(128)}, f32[8,16384]{1,0:T(8,128)S(1)}, s32[]{:T(128)}, bf16[8,256,4096]{2,1,0:T(8,128)(2,1)}, ...), condition=%wide.region_3.4_spmd, body=%wide.region_2.3_spmd.sunk | while | flops 1077936128 | bytes 29851780 | solution.py:33
  147.9 3.1 constant_dynamic-slice_fusion.4
  151.0 3.3 copy.84
  154.6 2.4 convolution_convert_fusion.2
  157.0 8.9 %fusion.31 = f32[4,64,64]{2,1,0:T(8,128)S(1)} fusion(bf16[256,64,64,1]{0,2,1,3:T(8,128)(2,1)S(1)} %bitcast.76, bf16[256,64,4,64]{0,3,2,1:T(8,128)(2,1)S(1)} %convolution_convert_fusion.2), kind=kOutput, calls=%fused_computation.8.clone.1 | convolution fusion | flops 536870912 | bytes 10551296 | tf_op jit(solution)/shard_map/while/body/dot_general | solution.py:17
  167.4 0.9 gather_fusion.1
  168.9 1.5 broadcast_select_fusion
  170.4 41.4 %all-to-all-start.2 = ((f32[8,2,16384]{2,1,0:T(2,128)}), f32[8,2,16384]{2,1,0:T(2,128)S(1)}, u32[]{:S(2)}, u32[]{:S(2)}) async-start(f32[8,2,16384]{2,1,0:T(2,128)} %broadcast_select_fusion), calls=%async_computation.2 | async-start | bytes 2097152 | tf_op jit(solution)/shard_map/all_to_all | solution.py:89
  212.3 15.5 %all-to-all-done.2 = f32[8,2,16384]{2,1,0:T(2,128)S(1)} async-done(((f32[8,2,16384]{2,1,0:T(2,128)}), f32[8,2,16384]{2,1,0:T(2,128)S(1)}, u32[]{:S(2)}, u32[]{:S(2)}) %all-to-all-start.2) | async-done | bytes 1048608 | tf_op jit(solution)/shard_map/all_to_all | solution.py:89
  228.4 100.1 %all-to-all-start.1 = ((s32[16,1,2]{2,1,0:T(1,128)}), s32[16,1,2]{2,1,0:T(1,128)S(1)}, u32[]{:S(2)}, u32[]{:S(2)}) async-start(s32[16,1,2]{2,1,0:T(1,128)} %bitcast.12), calls=%async_computation.1 | async-start | bytes 16384 | tf_op jit(solution)/shard_map/all_to_all | solution.py:101
  328.6 2.4 bitcast_select_fusion
  331.0 5.1 %all-to-all-done.1 = s32[16,1,2]{2,1,0:T(1,128)S(1)} async-done(((s32[16,1,2]{2,1,0:T(1,128)}), s32[16,1,2]{2,1,0:T(1,128)S(1)}, u32[]{:S(2)}, u32[]{:S(2)}) %all-to-all-start.1) | async-done | bytes 160 | tf_op jit(solution)/shard_map/all_to_all | solution.py:101
  336.0 3.7 all-to-all-start.3
  341.1 27.5 %all-to-all-done.3 = f32[16,2,16384]{2,1,0:T(2,128)S(1)} async-done(((f32[16,2,16384]{2,1,0:T(2,128)}), f32[16,2,16384]{2,1,0:T(2,128)S(1)}, u32[]{:S(2)}, u32[]{:S(2)}) %all-to-all-start.3) | async-done | bytes 2097184 | tf_op jit(solution)/shard_map/all_to_all | solution.py:100
  368.6 2.4 reshape.193
  371.0 4.4 %scatter_custom_fusion = f32[32,16384]{1,0:T(8,128)S(1)} fusion(s32[32]{0:T(128)S(1)} %fusion.16, f32[32,16384]{1,0:T(8,128)} %reshape.193, f32[]{:T(128)} %constant.97.clone.1), kind=kCustom, calls=%fused_computation.13 | custom fusion | flops 524288 | bytes 2097664 | tf_op jit(solution)/shard_map/scatter-add | solution.py:105
  375.4 3.0 reshape.148
  378.5 7.4 %copy.67 = f32[4,4,64,8,64]{4,3,2,1,0:T(8,128)} copy(f32[4,4,64,8,64]{4,2,0,3,1:T(8,128)} %bitcast.77) | data formatting | bytes 4194304 | tf_op jit(solution)/shard_map/transpose | solution.py:106
  385.9 4.8 %reshape.149 = f32[4,256,512]{2,1,0:T(8,128)} reshape(f32[4,4,64,8,64]{4,3,2,1,0:T(8,128)} %copy.67) | data formatting | bytes 4194304 | tf_op jit(solution)/shard_map/reshape | solution.py:107
  (56 shorter events, 13.3 us)
Async XLA Ops:
  6.5 116.9 %all-gather.2.cloned.1.call-start = ((), (), s32[]{:S(2)}) async-start(), calls=%async_computation.4 | async-start | bytes 17825792 | tf_op jit(solution)/shard_map/all_gather | solution.py:64
  10.9 159.5 %all-to-all-start = ((s32[8,2,2]{1,2,0:T(2,128)}), s32[8,2,2]{1,2,0:T(2,128)S(1)}, u32[]{:S(2)}, u32[]{:S(2)}) async-start(s32[8,2,2]{1,2,0:T(2,128)} %copy.61), calls=%async_computation | async-start | bytes 16384 | tf_op jit(solution)/shard_map/all_to_all | solution.py:90
  170.4 57.4 %all-to-all-start.2 = ((f32[8,2,16384]{2,1,0:T(2,128)}), f32[8,2,16384]{2,1,0:T(2,128)S(1)}, u32[]{:S(2)}, u32[]{:S(2)}) async-start(f32[8,2,16384]{2,1,0:T(2,128)} %broadcast_select_fusion), calls=%async_computation.2 | async-start | bytes 2097152 | tf_op jit(solution)/shard_map/all_to_all | solution.py:89
  228.4 107.7 %all-to-all-start.1 = ((s32[16,1,2]{2,1,0:T(1,128)}), s32[16,1,2]{2,1,0:T(1,128)S(1)}, u32[]{:S(2)}, u32[]{:S(2)}) async-start(s32[16,1,2]{2,1,0:T(1,128)} %bitcast.12), calls=%async_computation.1 | async-start | bytes 16384 | tf_op jit(solution)/shard_map/all_to_all | solution.py:101
  336.0 32.6 %all-to-all-start.3 = ((f32[16,2,16384]{2,1,0:T(2,128)}), f32[16,2,16384]{2,1,0:T(2,128)S(1)}, u32[]{:S(2)}, u32[]{:S(2)}) async-start(f32[16,2,16384]{2,1,0:T(2,128)} %bitcast_select_fusion), calls=%async_computation.3 | async-start | bytes 4194304 | tf_op jit(solution)/shard_map/all_to_all | solution.py:100
Sparse Core Ops, SparseCore 0:
  9.5 113.8 all-gather.1
where the time goes:
time: 400 us; the launch traced here: 398 us
  waiting for transfers between devices  156 us (39%)
  starting transfers between devices  150 us (38%)
  local copies, waits for them, and re-layouts  53.3 us (13%)
  between operations  13.5 us (3%)
  other arithmetic  12.1 us (3%)
  matrix products  11.3 us (3%)
    all_gather x1, waiting for transfers between devices, local(): portion = lax.all_gather(density, 'wide', axis=1, tiled=True)  107 us
    all_to_all x1, starting transfers between devices, local(): lax.all_to_all(forwarded_codes, 'wide', split_axis=0, concat_axis=0, tile...  100 us
    all_to_all x1, starting transfers between devices, local(): lax.all_to_all(values, 'narrow', split_axis=0, concat_axis=0, tiled=True)  41.4 us
    all_to_all x1, waiting for transfers between devices, local(): lax.all_to_all(forwarded, 'wide', split_axis=0, concat_axis=0, tiled=True)  27.5 us
    gather x24, local copies, waits for them, and re-layouts  23.1 us
    all_to_all x1, waiting for transfers between devices, local(): lax.all_to_all(values, 'narrow', split_axis=0, concat_axis=0, tiled=True)  15.5 us
    dot_general x1, matrix products, block_term(): lax.dot_general(halves, coef_mat, (((0, 3), (0, 1)), ((), ())), preferred...  8.89 us
  transfers between devices with their start and end apart: 5, of which 4 were waited for; matrix products, arithmetic and copies ran while one was open for 14% of the time, Pallas kernels for 0%

commit v1 on v0

v1 whole, which is shorter than its diff:
```python
import jax
import jax.numpy as jnp
from jax import lax
from jax.experimental import pallas as pl
from jax.experimental.pallas import tpu as pltpu
from jax.sharding import PartitionSpec as P

BF = 64
AUXP = 256
NDM = 4
SLOTS = 8
N_WIDE = 16
N_NARROW = 8
BF16 = jnp.bfloat16
F32 = jnp.float32
MESH = pl.DeviceIdType.MESH
NT = (((1,), (1,)), ((), ()))
NN = (((1,), (0,)), ((), ()))


def iota(shape, dim):
    return lax.broadcasted_iota(jnp.int32, shape, dim)


def one_hot(hit):
    return jnp.where(hit, 1.0, 0.0).astype(BF16)


def build_info(blocks, live):
    lane = iota((8, 128), 1)
    row = iota((8, 128), 0)
    info = jnp.where(row == 0, -1, 0)
    alive = lane * 0 + live[0]
    for t in range(SLOTS):
        r, c = blocks[t, 0], blocks[t, 1]
        hit = (lane == lax.div(c, 4)) & (t < alive)
        info = jnp.where(hit & (row == 0), r * 64 + c, info)
        info = jnp.where(hit & (row == 1), t, info)
    return info


def pack_block(dens, code):
    code = jnp.maximum(code, 0)
    r, c = lax.div(code, 64), lax.rem(code, 64)
    pair = dens[lax.rem(c, 4), lax.div(lax.rem(r, 8), 2)].astype(F32)
    lane = iota((BF, 128), 1)
    odd = lane * 0 + lax.rem(r, 2) == 1
    parts = []
    for d in range(NDM):
        turned = pltpu.roll(pair[d], BF, 1)
        if d % 2 == 0:
            parts.append(jnp.where(odd, turned, pair[d]))
        else:
            parts.append(jnp.where(odd, pair[d], turned))
    low = lane < BF
    first = jnp.where(low, parts[0], parts[1])
    second = jnp.where(low, parts[2], parts[3])
    return jnp.concatenate([first, second], axis=1).astype(BF16)


def spread_block(block, perm, dz):
    tall = jnp.concatenate([block] * 4, axis=0)
    turned = lax.dot_general(perm[...], tall, NT, preferred_element_type=F32).astype(BF16)
    part = iota((256, 256), 1) // BF
    for q in range(4):
        dz[q] = jnp.where(part == q, turned, jnp.zeros_like(turned))


def task_term(coef, dz, half):
    groups = 16
    tall = jnp.concatenate([coef[:, g * 256:(g + 1) * 256] for g in range(groups)], axis=0)
    for q in range(4):
        rows = lax.dot_general(dz[q], tall, NT, preferred_element_type=F32).astype(BF16)
        for g in range(groups):
            half[g * 4 + q] = rows[:, g * 256:(g + 1) * 256]
    left = jnp.concatenate(
        [half[:, j * 16:(j + 1) * 16, :].reshape(BF * 16, AUXP) for j in range(16)], axis=1
    )
    right = jnp.concatenate([coef[:, j * 256:(j + 1) * 256] for j in range(16)], axis=0)
    full = lax.dot_general(left, right, NN, preferred_element_type=F32)
    full = full.reshape(BF, 2, 8, 256)
    both = full[:, 0, :, :128] + full[:, 1, :, 128:]
    keep = iota((8, 128), 0) // 4 == iota((8, 128), 1) // BF
    both = jnp.where(keep[None], both, 0.0)
    return both + pltpu.roll(pltpu.roll(both, BF, 2), 4, 1)


def slot_layout(folded, pick):
    flat = folded.reshape(BF * 8, 128).astype(BF16)
    even = lax.dot_general(pick[0], flat, NN, preferred_element_type=F32)
    odd = lax.dot_general(pick[1], flat, NN, preferred_element_type=F32)
    return jnp.where(iota((128, 128), 1) < BF, even, odd).astype(BF16)


def exchange_kernel(
    dens_hbm, coef_hbm, blocks, live, recv, meta,
    coef, dens, info, own, codes, codes_sm, dsend, dblk, dz, perm, pick, half, terms, slots,
    coef_sem, dens_sem, small_sem, code_send, code_recv, meta_send, meta_recv, d_send, d_recv, t_send, t_recv,
):
    w = lax.axis_index("wide")
    n = lax.axis_index("narrow")
    src_n = w // 2

    def dens_copy(k):
        i, j = k // 4, k % 4
        return pltpu.make_async_copy(
            dens_hbm.at[:, pl.ds(i * BF, BF), pl.ds(j * 128, 128)], dens.at[i, j], dens_sem.at[k]
        )

    for k in range(16):
        dens_copy(k).start()
    for t in range(SLOTS):
        pltpu.make_async_copy(coef_hbm.at[t], coef.at[t], coef_sem.at[t]).start()

    info[...] = build_info(blocks, live)
    own_copy = pltpu.make_async_copy(info, own, small_sem.at[0])
    own_copy.start()

    barrier = pltpu.get_barrier_semaphore()

    def greet_peer(k, carry):
        pl.semaphore_signal(barrier, inc=1, device_id=(lax.rem(w + k, N_WIDE), n), device_id_type=MESH)
        return carry

    lax.fori_loop(1, N_WIDE, greet_peer, 0)

    def greet_source(k, carry):
        @pl.when(jnp.logical_or(k != w, src_n != n))
        def _():
            pl.semaphore_signal(barrier, inc=1, device_id=(k, src_n), device_id_type=MESH)
        return carry

    lax.fori_loop(0, N_WIDE, greet_source, 0)

    @pl.when(src_n == n)
    def _():
        pl.semaphore_wait(barrier, 2 * N_WIDE - 2)

    @pl.when(src_n != n)
    def _():
        pl.semaphore_wait(barrier, 2 * N_WIDE - 1)

    def code_copy(k):
        peer = lax.rem(w + k, N_WIDE)
        return pltpu.make_async_remote_copy(
            src_ref=info, dst_ref=codes.at[w], send_sem=code_send.at[k], recv_sem=code_recv.at[w],
            device_id=(peer, n), device_id_type=MESH,
        )

    def send_code(k, carry):
        code_copy(k).start()
        return carry

    lax.fori_loop(1, N_WIDE, send_code, 0)
    codes[w] = info[...]

    def meta_copy(j):
        return pltpu.make_async_remote_copy(
            src_ref=info, dst_ref=meta.at[w], send_sem=meta_send.at[j], recv_sem=meta_recv.at[w],
            device_id=(2 * n + j // N_NARROW, j % N_NARROW), device_id_type=MESH,
        )

    def is_self(j):
        return jnp.logical_and(2 * n + j // N_NARROW == w, j % N_NARROW == n)

    def send_meta(j, carry):
        @pl.when(is_self(j))
        def _():
            pltpu.make_async_copy(info, meta.at[w], meta_recv.at[w]).start()

        @pl.when(jnp.logical_not(is_self(j)))
        def _():
            meta_copy(j).start()
        return carry

    i, k = iota((256, 256), 0), iota((256, 256), 1)
    perm[...] = one_hot(k == (i % 4) * BF + i // 4)
    i, k = iota((128, 512), 0), iota((128, 512), 1)
    pick[0] = one_hot(k == (i % BF) * 8 + i // BF)
    pick[1] = one_hot(k == (i % BF) * 8 + 6 + i // BF)

    def wait_code(k, carry):
        peer = lax.rem(w + k, N_WIDE)
        pltpu.make_async_copy(info, codes.at[peer], code_recv.at[peer]).wait()
        return carry

    lax.fori_loop(1, N_WIDE, wait_code, 0)
    codes_copy = pltpu.make_async_copy(codes, codes_sm, small_sem.at[1])
    codes_copy.start()
    lax.fori_loop(0, N_WIDE, send_meta, 0)
    for k in range(16):
        dens_copy(k).wait()
    own_copy.wait()
    codes_copy.wait()

    def block_copy(k):
        peer = lax.rem(w + k, N_WIDE)
        return pltpu.make_async_remote_copy(
            src_ref=dsend.at[k], dst_ref=dblk.at[w], send_sem=d_send.at[k], recv_sem=d_recv.at[w],
            device_id=(peer, n), device_id_type=MESH,
        )

    def send_block(k, carry):
        peer = lax.rem(w + k, N_WIDE)
        dsend[k] = pack_block(dens, codes_sm[peer, 0, w])
        block_copy(k).start()
        return carry

    lax.fori_loop(1, N_WIDE, send_block, 0)
    dblk[w] = pack_block(dens, codes_sm[w, 0, w])

    def wait_block(k, carry):
        peer = lax.rem(w + k, N_WIDE)
        pltpu.make_async_copy(dsend.at[k], dblk.at[peer], d_recv.at[peer]).wait()
        return carry

    lax.fori_loop(1, N_WIDE, wait_block, 0)

    def run_task(t, carry):
        pltpu.make_async_copy(coef_hbm.at[t], coef.at[t], coef_sem.at[t]).wait()
        spread_block(dblk[lax.div(blocks[t, 1], 4)], perm, dz)
        terms[t] = slot_layout(task_term(coef.at[t], dz, half), pick)
        return carry

    lax.fori_loop(0, SLOTS, run_task, 0)

    def term_copy(j):
        return pltpu.make_async_remote_copy(
            src_ref=slots.at[j % N_NARROW], dst_ref=recv.at[w], send_sem=t_send.at[j], recv_sem=t_recv.at[w],
            device_id=(2 * n + j // N_NARROW, j % N_NARROW), device_id_type=MESH,
        )

    def send_term(k, carry):
        q = lax.rem(n + k, N_NARROW)
        slots[q, 0] = terms[own[1, 2 * q]]
        slots[q, 1] = terms[own[1, 2 * q + 1]]
        for a in range(2):
            j = a * N_NARROW + q

            @pl.when(is_self(j))
            def _():
                pltpu.make_async_copy(slots.at[q], recv.at[w], t_recv.at[w]).start()

            @pl.when(jnp.logical_not(is_self(j)))
            def _():
                term_copy(j).start()
        return carry

    lax.fori_loop(0, N_NARROW, send_term, 0)

    def wait_in(k, carry):
        pltpu.make_async_copy(info, meta.at[k], meta_recv.at[k]).wait()
        pltpu.make_async_copy(slots.at[0], recv.at[k], t_recv.at[k]).wait()
        return carry

    lax.fori_loop(0, N_WIDE, wait_in, 0)

    def wait_out(j, carry):
        @pl.when(j > 0)
        def _():
            code_copy(j).wait_send()
            block_copy(j).wait_send()

        @pl.when(jnp.logical_not(is_self(j)))
        def _():
            meta_copy(j).wait_send()
            term_copy(j).wait_send()
        return carry

    lax.fori_loop(0, N_WIDE, wait_out, 0)


def scatter_kernel(meta, recv, out):
    wide = lax.axis_index("wide")
    narrow = lax.axis_index("narrow")
    out[...] = jnp.zeros_like(out)
    lane_half = iota((128, 128), 1) // BF

    def add_slot(k, carry):
        source, b = k // 2, k % 2
        code = meta[source, 0, 2 * narrow + b]
        r, c = code // 64, code % 64

        @pl.when(jnp.logical_and(code >= 0, r // 4 == wide))
        def _():
            here = recv[source, b].astype(F32)
            turned = pltpu.roll(here, BF, 1)
            odd = c % 2
            keep = lane_half == odd
            rows = pl.multiple_of((r % 4) * BF, BF)
            cols = pl.multiple_of(((c % 8) // 2) * 128, 128)
            for high in range(2):
                part = jnp.where(keep, jnp.where(odd == high, here, turned), 0.0)
                for low in range(2):
                    at = (2 * high + low, pl.ds(rows, BF), pl.ds(cols, 128))
                    out[at] = out[at] + part[low * BF:(low + 1) * BF]
        return carry

    lax.fori_loop(0, 2 * N_WIDE, add_slot, 0)


def local(density, coefficients, task_blocks, task_live):
    any_space = pl.BlockSpec(memory_space=pl.ANY)
    smem = pl.BlockSpec(memory_space=pltpu.SMEM)
    vmem = pl.BlockSpec(memory_space=pltpu.VMEM)
    dma = pltpu.SemaphoreType.DMA
    recv, meta = pl.pallas_call(
        exchange_kernel,
        out_shape=[
            jax.ShapeDtypeStruct((N_WIDE, 2, 128, 128), BF16),
            jax.ShapeDtypeStruct((N_WIDE, 8, 128), jnp.int32),
        ],
        in_specs=[any_space, any_space, smem, smem],
        out_specs=[any_space, any_space],
        scratch_shapes=[
            pltpu.VMEM((SLOTS, AUXP, BF * BF), BF16),
            pltpu.VMEM((4, 4, NDM, BF, 128), BF16),
            pltpu.VMEM((8, 128), jnp.int32),
            pltpu.SMEM((8, 128), jnp.int32),
            pltpu.VMEM((N_WIDE, 8, 128), jnp.int32),
            pltpu.SMEM((N_WIDE, 8, 128), jnp.int32),
            pltpu.VMEM((N_WIDE, BF, 256), BF16),
            pltpu.VMEM((N_WIDE, BF, 256), BF16),
            pltpu.VMEM((4, 256, 256), BF16),
            pltpu.VMEM((256, 256), BF16),
            pltpu.VMEM((2, 128, 512), BF16),
            pltpu.VMEM((BF, 256, AUXP), BF16),
            pltpu.VMEM((SLOTS, 128, 128), BF16),
            pltpu.VMEM((N_NARROW, 2, 128, 128), BF16),
            dma((SLOTS,)), dma((16,)), dma((2,)),
            dma((N_WIDE,)), dma((N_WIDE,)), dma((N_WIDE,)), dma((N_WIDE,)),
            dma((N_WIDE,)), dma((N_WIDE,)), dma((N_WIDE,)), dma((N_WIDE,)),
        ],
        compiler_params=pltpu.CompilerParams(
            collective_id=0, has_side_effects=True, vmem_limit_bytes=56 * 2**20
        ),
        name="exchange",
    )(density, coefficients, task_blocks, task_live)
    return pl.pallas_call(
        scatter_kernel,
        out_shape=jax.ShapeDtypeStruct(density.shape, F32),
        in_specs=[smem, vmem],
        out_specs=vmem,
        compiler_params=pltpu.CompilerParams(vmem_limit_bytes=32 * 2**20),
        name="scatter",
    )(meta, recv)


def solution(mesh):
    in_specs = (
        P(None, "wide", "narrow"),
        P(("wide", "narrow"), None, None),
        P(("wide", "narrow"), None),
        P(("wide", "narrow")),
    )
    out_specs = P(None, "wide", "narrow")
    return jax.shard_map(local, mesh=mesh, in_specs=in_specs, out_specs=out_specs, check_vma=False)
```

time: 400 us -> 95.1 us (0.24)
  the two profiles are of different devices: /device:TPU:0 before, /device:TPU:25 now
where the time goes in v1:
time: 95.1 us; the launch traced here: 94.9 us
  Pallas kernels  90.8 us (95%)
  local copies, waits for them, and re-layouts  3.4 us (4%)
    pallas_call x1, Pallas kernels, local(): pl.pallas_call(exchange_kernel, out_shape=[jax.ShapeDtypeStruct((N_WIDE,...  86.3 us
    pallas_call x1, Pallas kernels, local(): pl.pallas_call(scatter_kernel, out_shape=jax.ShapeDtypeStruct(density.sha...  4.43 us
    unnamed x5, local copies, waits for them, and re-layouts  3.4 us

profile of v1, /device:TPU:25, one launch (start us, length us, event | category | flops | bytes accessed | tf_op | source)
XLA Modules:
  0.0 94.9 jit_solution(15431702315053711668)
XLA Ops:
  0.7 1.3 %copy.5.blocks = s32[8,2]{1,0:T(8,128)} copy(s32[8,2]{0,1:T(2,128)} %param.6) | data formatting | bytes 128 | tf_op args[2]
  2.0 86.3 %exchange.1 = (bf16[16,2,128,128]{3,2,1,0:T(8,128)(2,1)}, s32[16,8,128]{2,1,0:T(8,128)}) custom-call(bf16[4,256,512]{2,1,0:T(8,128)(2,1)} %dens_hbm.1, bf16[8,256,4096]{2,1,0:T(8,128)(2,1)} %coef_hbm.1, s32[8,2]{1,0:T(8,128)} %copy.5.blocks, s32[1]{0:T(128)S(6)} %copy.6.live), custom_call_target="tpu_custom_call" | custom-call | tf_op jit(solution)/shard_map/exchange/pallas_call | solution.py:307
  88.4 0.0 copy-start
  88.4 1.2 %copy-done = bf16[16,2,128,128]{3,2,1,0:T(8,128)(2,1)S(1)} copy-done((bf16[16,2,128,128]{3,2,1,0:T(8,128)(2,1)S(1)}, bf16[16,2,128,128]{3,2,1,0:T(8,128)(2,1)}, u32[]{:S(2)}) %copy-start) | copy-done | bytes 1048600
  89.6 0.0 copy-start.1
  89.6 0.8 copy-done.1
  90.4 4.4 %scatter.1 = f32[4,256,512]{2,1,0:T(8,128)} custom-call(s32[16,8,128]{2,1,0:T(8,128)S(1)} %copy-done.1, bf16[16,2,128,128]{3,2,1,0:T(8,128)(2,1)S(1)} %copy-done), custom_call_target="tpu_custom_call" | custom-call | tf_op jit(solution)/shard_map/scatter/pallas_call | solution.py:339
Async XLA Ops:
  88.4 1.2 %copy-start = (bf16[16,2,128,128]{3,2,1,0:T(8,128)(2,1)S(1)}, bf16[16,2,128,128]{3,2,1,0:T(8,128)(2,1)}, u32[]{:S(2)}) copy-start(bf16[16,2,128,128]{3,2,1,0:T(8,128)(2,1)} %get-tuple-element.8.recv) | copy-start | bytes 3145732
  89.6 0.8 copy-start.1

commit v2 on v1

v2 whole, which is shorter than its diff:
```python
import jax
import jax.numpy as jnp
from jax import lax
from jax.experimental import pallas as pl
from jax.experimental.pallas import tpu as pltpu
from jax.sharding import PartitionSpec as P

BF = 64
AUXP = 256
NDM = 4
SLOTS = 8
N_WIDE = 16
N_NARROW = 8
BF16 = jnp.bfloat16
F32 = jnp.float32
MESH = pl.DeviceIdType.MESH
PASSES = ((0, 10), (10, 6))
NT = (((1,), (1,)), ((), ()))
NN = (((1,), (0,)), ((), ()))


def iota(shape, dim):
    return lax.broadcasted_iota(jnp.int32, shape, dim)


def one_hot(hit):
    return jnp.where(hit, 1.0, 0.0).astype(BF16)


def build_info(blocks, live):
    lane = iota((8, 128), 1)
    row = iota((8, 128), 0)
    info = jnp.where(row == 0, -1, 0)
    alive = lane * 0 + live[0]
    for t in range(SLOTS):
        r, c = blocks[0, t], blocks[1, t]
        hit = (lane == lax.div(c, 4)) & (t < alive)
        info = jnp.where(hit & (row == 0), r * 64 + c, info)
        info = jnp.where(hit & (row == 1), t, info)
    return info


def pack_block(dens, code):
    code = jnp.maximum(code, 0)
    r, c = lax.div(code, 64), lax.rem(code, 64)
    pair = dens[lax.rem(c, 4), lax.div(lax.rem(r, 8), 2)].astype(F32)
    lane = iota((BF, 128), 1)
    odd = lane * 0 + lax.rem(r, 2) == 1
    parts = []
    for d in range(NDM):
        turned = pltpu.roll(pair[d], BF, 1)
        if d % 2 == 0:
            parts.append(jnp.where(odd, turned, pair[d]))
        else:
            parts.append(jnp.where(odd, pair[d], turned))
    low = lane < BF
    first = jnp.where(low, parts[0], parts[1])
    second = jnp.where(low, parts[2], parts[3])
    return jnp.concatenate([first, second], axis=1).astype(BF16)


def spread_block(block, perm, dz):
    tall = jnp.concatenate([block] * 4, axis=0)
    turned = lax.dot_general(perm[...], tall, NT, preferred_element_type=F32).astype(BF16)
    part = iota((256, 256), 1) // BF
    for q in range(4):
        dz[q] = jnp.where(part == q, turned, jnp.zeros_like(turned))


def first_step(coef, dz, half, start, groups):
    tall = jnp.concatenate(
        [coef[:, g * 256:(g + 1) * 256] for g in range(start, start + groups)], axis=0
    )
    for q in range(4):
        rows = lax.dot_general(dz[q], tall, NT, preferred_element_type=F32).astype(BF16)
        for g in range(groups):
            half[g * 4 + q] = rows[:, g * 256:(g + 1) * 256]


def second_step(coef, half, groups):
    m = 4 * groups
    left = jnp.concatenate(
        [half[0:m, j * 16:(j + 1) * 16, :].reshape(m * 16, AUXP) for j in range(16)], axis=1
    )
    right = jnp.concatenate([coef[:, j * 256:(j + 1) * 256] for j in range(16)], axis=0)
    full = lax.dot_general(left, right, NN, preferred_element_type=F32)
    full = full.reshape(m, 2, 8, 256)
    both = full[:, 0, :, :128] + full[:, 1, :, 128:]
    keep = iota((8, 128), 0) // 4 == iota((8, 128), 1) // BF
    both = jnp.where(keep[None], both, 0.0)
    folded = both + pltpu.roll(pltpu.roll(both, BF, 2), 4, 1)
    flat = folded.reshape(m * 8, 128).astype(BF16)
    i, k = iota((2 * m, m * 8), 0), iota((2 * m, m * 8), 1)
    even = one_hot(k == (i % m) * 8 + i // m)
    odd = one_hot(k == (i % m) * 8 + 6 + i // m)
    even = lax.dot_general(even, flat, NN, preferred_element_type=F32)
    odd = lax.dot_general(odd, flat, NN, preferred_element_type=F32)
    return jnp.where(iota((2 * m, 128), 1) < BF, even, odd).astype(BF16)


def label(code):
    lane = iota((16, 128), 1)
    code = lane * 0 + code
    r, c = lax.div(code, jnp.full_like(code, 64)), lax.rem(code, jnp.full_like(code, 64))
    value = jnp.where(lane == 0, r, jnp.where(lane == 1, c, jnp.where(code >= 0, 1, 0)))
    return value.astype(F32).astype(BF16)


def exchange_kernel(
    dens_hbm, coef_hbm, blocks, live, *refs
):
    count = len(PASSES)
    recvs, refs = refs[:count], refs[count:]
    terms, slots, refs = refs[:count], refs[count:2 * count], refs[2 * count:]
    (
        coef, dens, info, own, codes, codes_sm, dsend, dblk, dz, perm, half, coef_sem, dens_sem, small_sem,
        code_send, code_recv, d_send, d_recv, t_send, t_recv,
    ) = refs
    w = lax.axis_index("wide")
    n = lax.axis_index("narrow")
    src_n = lax.div(w, 2)

    def dens_copy(k):
        i, j = k // 4, k % 4
        return pltpu.make_async_copy(
            dens_hbm.at[:, pl.ds(i * BF, BF), pl.ds(j * 128, 128)], dens.at[i, j], dens_sem.at[k]
        )

    for k in range(16):
        dens_copy(k).start()
    info[...] = build_info(blocks, live)
    own_copy = pltpu.make_async_copy(info, own, small_sem.at[0])
    own_copy.start()

    barrier = pltpu.get_barrier_semaphore()

    for k in range(1, N_WIDE):
        pl.semaphore_signal(barrier, inc=1, device_id=(lax.rem(w + k, N_WIDE), n), device_id_type=MESH)
    for k in range(N_WIDE):

        @pl.when(jnp.logical_or(k != w, src_n != n))
        def _():
            pl.semaphore_signal(barrier, inc=1, device_id=(k, src_n), device_id_type=MESH)

    @pl.when(src_n == n)
    def _():
        pl.semaphore_wait(barrier, 2 * N_WIDE - 2)

    @pl.when(src_n != n)
    def _():
        pl.semaphore_wait(barrier, 2 * N_WIDE - 1)

    def code_copy(k):
        peer = lax.rem(w + k, N_WIDE)
        return pltpu.make_async_remote_copy(
            src_ref=info, dst_ref=codes.at[w], send_sem=code_send.at[k], recv_sem=code_recv.at[w],
            device_id=(peer, n), device_id_type=MESH,
        )

    for k in range(1, N_WIDE):
        code_copy(k).start()
    codes[w] = info[...]

    i, k = iota((256, 256), 0), iota((256, 256), 1)
    perm[...] = one_hot(k == (i % 4) * BF + i // 4)

    for k in range(1, N_WIDE):
        peer = lax.rem(w + k, N_WIDE)
        pltpu.make_async_copy(info, codes.at[peer], code_recv.at[peer]).wait()
    codes_copy = pltpu.make_async_copy(codes.at[:, pl.ds(0, 1), :], codes_sm, small_sem.at[1])
    codes_copy.start()
    for k in range(16):
        dens_copy(k).wait()
    own_copy.wait()
    codes_copy.wait()

    def block_copy(k):
        peer = lax.rem(w + k, N_WIDE)
        return pltpu.make_async_remote_copy(
            src_ref=dsend.at[k], dst_ref=dblk.at[w], send_sem=d_send.at[k], recv_sem=d_recv.at[w],
            device_id=(peer, n), device_id_type=MESH,
        )

    for k in range(1, N_WIDE):
        dsend[k] = pack_block(dens, codes_sm[lax.rem(w + k, N_WIDE), 0, w])
        block_copy(k).start()
    dblk[w] = pack_block(dens, codes_sm[w, 0, w])
    for t in range(SLOTS):
        pltpu.make_async_copy(coef_hbm.at[t], coef.at[t], coef_sem.at[t]).start()
    for k in range(1, N_WIDE):
        peer = lax.rem(w + k, N_WIDE)
        pltpu.make_async_copy(dsend.at[k], dblk.at[peer], d_recv.at[peer]).wait()

    def wait_coef(t):
        pltpu.make_async_copy(coef_hbm.at[t], coef.at[t], coef_sem.at[t]).wait()

    def term_copy(i, a, q):
        return pltpu.make_async_remote_copy(
            src_ref=slots[i].at[q], dst_ref=recvs[i].at[w],
            send_sem=t_send.at[i, a, q], recv_sem=t_recv.at[i, w],
            device_id=(2 * n + a, q), device_id_type=MESH,
        )

    def run_pass(i):
        start, groups = PASSES[i]
        m = 4 * groups

        def task(t, carry):
            if i == 0:
                wait_coef(t)
                spread_block(dblk[lax.div(blocks[1, t], 4)], perm, dz.at[t])
            first_step(coef.at[t], dz.at[t], half, start, groups)
            terms[i][t] = second_step(coef.at[t], half, groups)
            return carry

        lax.fori_loop(0, SLOTS, task, 0)
        for k in range(N_NARROW):
            q = lax.rem(n + k, N_NARROW)
            for b in range(2):
                slots[i][q, b, 0:2 * m] = terms[i][own[1, 2 * q + b]]
                if i == 0:
                    slots[i][q, b, 2 * m:2 * m + 16] = label(own[0, 2 * q + b])
            for a in range(2):
                if k > 0:
                    term_copy(i, a, q).start()
                    continue

                @pl.when(2 * n + a == w)
                def _():
                    pltpu.make_async_copy(slots[i].at[q], recvs[i].at[w], t_recv.at[i, w]).start()

                @pl.when(2 * n + a != w)
                def _():
                    term_copy(i, a, q).start()

    for i in range(count):
        run_pass(i)

    def wait_sent(i):
        for a in range(2):
            for k in range(N_NARROW):
                q = lax.rem(n + k, N_NARROW)
                if k > 0:
                    term_copy(i, a, q).wait_send()
                    continue

                @pl.when(2 * n + a != w)
                def _():
                    term_copy(i, a, q).wait_send()

    for k in range(1, N_WIDE):
        code_copy(k).wait_send()
        block_copy(k).wait_send()
    for i in range(count):
        for k in range(N_WIDE):
            pltpu.make_async_copy(slots[i].at[0], recvs[i].at[k], t_recv.at[i, k]).wait()
        wait_sent(i)


def scatter_kernel(*refs):
    count = len(PASSES)
    recv_hbm, out, recv, (found, table, sem) = refs[:count], refs[count], refs[count + 1:2 * count + 1], refs[2 * count + 1:]
    wide = lax.axis_index("wide")
    copies = [pltpu.make_async_copy(recv_hbm[i], recv[i], sem.at[i]) for i in range(count)]
    for copy in copies:
        copy.start()
    copies[0].wait()
    m = 4 * PASSES[0][1]
    found[...] = recv[0][:, :, 2 * m:2 * m + 16, :].astype(F32).astype(jnp.int32)
    table_copy = pltpu.make_async_copy(found.at[:, :, pl.ds(0, 1), :], table, sem.at[count])
    table_copy.start()
    out[...] = jnp.zeros_like(out)
    for copy in copies[1:]:
        copy.wait()
    table_copy.wait()

    def add_slot(k, carry):
        source, b = lax.div(k, 2), lax.rem(k, 2)
        r, c, there = (table[source, b, 0, lane] for lane in range(3))

        @pl.when(jnp.logical_and(there > 0, lax.div(r, 4) == wide))
        def _():
            odd = lax.rem(c, 2)
            rows = lax.rem(r, 4) * BF
            cols = lax.div(lax.rem(c, 8), 2) * 128
            for i in range(count):
                start, m = 4 * PASSES[i][0], 4 * PASSES[i][1]
                keep = iota((2 * m, 128), 1) // BF == odd
                here = recv[i][source, b, 0:2 * m].astype(F32)
                turned = pltpu.roll(here, BF, 1)
                for high in range(2):
                    part = jnp.where(keep, jnp.where(odd == high, here, turned), 0.0)
                    for low in range(2):
                        at = (2 * high + low, pl.ds(rows + start, m), pl.ds(cols, 128))
                        out[at] = out[at] + part[low * m:(low + 1) * m]
        return carry

    lax.fori_loop(0, 2 * N_WIDE, add_slot, 0)


def local(density, coefficients, task_blocks, task_live):
    any_space = pl.BlockSpec(memory_space=pl.ANY)
    smem = pl.BlockSpec(memory_space=pltpu.SMEM)
    dma = pltpu.SemaphoreType.DMA
    count = len(PASSES)
    sizes = [8 * groups for _, groups in PASSES]
    sent = [size + 16 * (i == 0) for i, size in enumerate(sizes)]
    recv = pl.pallas_call(
        exchange_kernel,
        out_shape=[jax.ShapeDtypeStruct((N_WIDE, 2, size, 128), BF16) for size in sent],
        in_specs=[any_space, any_space, smem, smem],
        out_specs=[any_space] * count,
        scratch_shapes=[pltpu.VMEM((SLOTS, size, 128), BF16) for size in sizes]
        + [pltpu.VMEM((N_NARROW, 2, size, 128), BF16) for size in sent]
        + [
            pltpu.VMEM((SLOTS, AUXP, BF * BF), BF16),
            pltpu.VMEM((4, 4, NDM, BF, 128), BF16),
            pltpu.VMEM((8, 128), jnp.int32),
            pltpu.SMEM((8, 128), jnp.int32),
            pltpu.VMEM((N_WIDE, 8, 128), jnp.int32),
            pltpu.SMEM((N_WIDE, 1, 128), jnp.int32),
            pltpu.VMEM((N_WIDE, BF, 256), BF16),
            pltpu.VMEM((N_WIDE, BF, 256), BF16),
            pltpu.VMEM((SLOTS, 4, 256, 256), BF16),
            pltpu.VMEM((256, 256), BF16),
            pltpu.VMEM((max(sizes) // 2, 256, AUXP), BF16),
            dma((SLOTS,)), dma((16,)), dma((2,)),
            dma((N_WIDE,)), dma((N_WIDE,)), dma((N_WIDE,)), dma((N_WIDE,)),
            dma((count, 2, N_NARROW)), dma((count, N_WIDE)),
        ],
        compiler_params=pltpu.CompilerParams(
            collective_id=0, has_side_effects=True, vmem_limit_bytes=56 * 2**20
        ),
        name="exchange",
    )(density, coefficients, task_blocks.T, task_live)
    return pl.pallas_call(
        scatter_kernel,
        out_shape=jax.ShapeDtypeStruct(density.shape, F32),
        in_specs=[any_space] * count,
        out_specs=pl.BlockSpec(memory_space=pltpu.VMEM),
        scratch_shapes=[pltpu.VMEM((N_WIDE, 2, size, 128), BF16) for size in sent]
        + [
            pltpu.VMEM((N_WIDE, 2, 16, 128), jnp.int32),
            pltpu.SMEM((N_WIDE, 2, 1, 128), jnp.int32),
            dma((count + 1,)),
        ],
        compiler_params=pltpu.CompilerParams(vmem_limit_bytes=60 * 2**20),
        name="scatter",
    )(*recv)


def solution(mesh):
    in_specs = (
        P(None, "wide", "narrow"),
        P(("wide", "narrow"), None, None),
        P(("wide", "narrow"), None),
        P(("wide", "narrow")),
    )
    out_specs = P(None, "wide", "narrow")
    return jax.shard_map(local, mesh=mesh, in_specs=in_specs, out_specs=out_specs, check_vma=False)
```

time: 95.1 us -> 81.8 us (0.86)
  the two profiles are of different devices: /device:TPU:25 before, /device:TPU:97 now
where the time goes in v2:
time: 81.8 us; the launch traced here: 81.3 us
  Pallas kernels  80.6 us (99%)
    pallas_call x1, Pallas kernels, local(): pl.pallas_call(exchange_kernel, out_shape=[jax.ShapeDtypeStruct((N_WIDE,...  76 us
    pallas_call x1, Pallas kernels, local(): pl.pallas_call(scatter_kernel, out_shape=jax.ShapeDtypeStruct(density.sha...  4.6 us

profile of v2, /device:TPU:97, one launch (start us, length us, event | category | flops | bytes accessed | tf_op | source)
XLA Modules:
  0.0 81.3 jit_solution(11927590670308124072)
XLA Ops:
  0.7 76.0 %exchange.1 = (bf16[16,2,96,128]{3,2,1,0:T(8,128)(2,1)}, bf16[16,2,48,128]{3,2,1,0:T(8,128)(2,1)}) custom-call(bf16[4,256,512]{2,1,0:T(8,128)(2,1)} %dens_hbm.1, bf16[8,256,4096]{2,1,0:T(8,128)(2,1)} %coef_hbm.1, s32[2,8]{1,0:T(2,128)} %bitcast.1, s32[1]{0:T(128)S(6)} %copy.5.live), custom_call_target="tpu_custom_call" | custom-call | tf_op jit(solution)/shard_map/exchange/pallas_call | solution.py:308
  76.7 4.6 %scatter.1 = f32[4,256,512]{2,1,0:T(8,128)} custom-call(bf16[16,2,96,128]{3,2,1,0:T(8,128)(2,1)} %get-tuple-element.7.refs_0_, bf16[16,2,48,128]{3,2,1,0:T(8,128)(2,1)} %get-tuple-element.8.refs_1_), custom_call_target="tpu_custom_call" | custom-call | tf_op jit(solution)/shard_map/scatter/pallas_call | solution.py:336

commit v3 on v2

v3 whole, which is shorter than its diff:
```python
import jax
import jax.numpy as jnp
from jax import lax
from jax.experimental import pallas as pl
from jax.experimental.pallas import tpu as pltpu
from jax.sharding import PartitionSpec as P

BF = 64
AUXP = 256
NDM = 4
SLOTS = 8
N_WIDE = 16
N_NARROW = 8
BF16 = jnp.bfloat16
F32 = jnp.float32
MESH = pl.DeviceIdType.MESH
PASSES = ((0, 10), (10, 6))
NT = (((1,), (1,)), ((), ()))
NN = (((1,), (0,)), ((), ()))


def iota(shape, dim):
    return lax.broadcasted_iota(jnp.int32, shape, dim)


def one_hot(hit):
    return jnp.where(hit, 1.0, 0.0).astype(BF16)


def build_info(blocks, live):
    lane = iota((8, 128), 1)
    info = jnp.full((8, 128), -1, jnp.int32)
    alive = lane * 0 + live[0]
    for t in range(SLOTS):
        r, c = blocks[0, t], blocks[1, t]
        info = jnp.where((lane == lax.div(c, 4)) & (t < alive), r * 64 + c, info)
    return info


def build_plan(blocks, info, first):
    lane = iota((8, 128), 1)
    row = iota((8, 128), 0)
    stripes = [lax.div(blocks[1, t], 4) for t in range(SLOTS)]
    keys = [lax.rem(stripe + N_WIDE - first, N_WIDE) for stripe in stripes]
    plan = jnp.where(row == 0, info, 0)
    for t in range(SLOTS):
        place = sum((keys[u] < keys[t]).astype(jnp.int32) for u in range(SLOTS) if u != t)
        plan = jnp.where((row == 1) & (lane == stripes[t]), place, plan)
        plan = jnp.where((row == 2) & (lane == place), t, plan)
        plan = jnp.where((row == 3) & (lane == place), stripes[t], plan)
    return plan


def pack_block(dens, code):
    code = jnp.maximum(code, 0)
    r, c = lax.div(code, 64), lax.rem(code, 64)
    pair = dens[lax.rem(c, 4), lax.div(lax.rem(r, 8), 2)].astype(F32)
    lane = iota((BF, 128), 1)
    odd = lane * 0 + lax.rem(r, 2) == 1
    low = lane < BF
    halves = []
    for d in range(0, NDM, 2):
        stays = jnp.where(odd, pair[d + 1], pair[d])
        moves = pltpu.roll(jnp.where(odd, pair[d], pair[d + 1]), BF, 1)
        halves.append(jnp.where(odd == low, moves, stays))
    return jnp.concatenate(halves, axis=1).astype(BF16)


def spread_block(block, perm, dz):
    tall = jnp.concatenate([block] * 4, axis=0)
    turned = lax.dot_general(perm[...], tall, NT, preferred_element_type=F32).astype(BF16)
    part = iota((256, 256), 1) // BF
    for q in range(4):
        dz[q] = jnp.where(part == q, turned, jnp.zeros_like(turned))


def first_step(coef, t, dz, half, start, groups):
    tall = jnp.concatenate(
        [coef[t, :, g * 256:(g + 1) * 256] for g in range(start, start + groups)], axis=0
    )
    for q in range(4):
        rows = lax.dot_general(dz[q], tall, NT, preferred_element_type=F32).astype(BF16)
        for g in range(groups):
            half[g * 4 + q] = rows[:, g * 256:(g + 1) * 256]


def second_step(coef, t, half, groups):
    m = 4 * groups
    left = jnp.concatenate(
        [half[0:m, j * 16:(j + 1) * 16, :].reshape(m * 16, AUXP) for j in range(16)], axis=1
    )
    right = jnp.concatenate([coef[t, :, j * 256:(j + 1) * 256] for j in range(16)], axis=0)
    full = lax.dot_general(left, right, NN, preferred_element_type=F32)
    full = full.reshape(m, 2, 8, 256)
    both = full[:, 0, :, :128] + full[:, 1, :, 128:]
    keep = iota((8, 128), 0) // 4 == iota((8, 128), 1) // BF
    both = jnp.where(keep[None], both, 0.0)
    folded = both + pltpu.roll(pltpu.roll(both, BF, 2), 4, 1)
    flat = folded.reshape(m * 8, 128).astype(BF16)
    i, k = iota((2 * m, m * 8), 0), iota((2 * m, m * 8), 1)
    even = one_hot(k == (i % m) * 8 + i // m)
    odd = one_hot(k == (i % m) * 8 + 6 + i // m)
    even = lax.dot_general(even, flat, NN, preferred_element_type=F32)
    odd = lax.dot_general(odd, flat, NN, preferred_element_type=F32)
    return jnp.where(iota((2 * m, 128), 1) < BF, even, odd).astype(BF16)


def label(code):
    lane = iota((16, 128), 1)
    code = lane * 0 + code
    r, c = lax.div(code, jnp.full_like(code, 64)), lax.rem(code, jnp.full_like(code, 64))
    value = jnp.where(lane == 0, r, jnp.where(lane == 1, c, jnp.where(code >= 0, 1, 0)))
    return value.astype(F32).astype(BF16)


def exchange_kernel(
    dens_hbm, coef_hbm, blocks, live, *refs
):
    count = len(PASSES)
    recvs, (table, *refs) = refs[:count], refs[count:]
    terms, slots, refs = refs[:count], refs[count:2 * count], refs[2 * count:]
    (
        coef, dens, info, plan, own, codes, codes_sm, dsend, dblk, dz, perm, half, labels, found, coef_sem, dens_sem, small_sem,
        code_send, code_recv, d_send, d_recv, t_send, t_recv,
    ) = refs
    w = lax.axis_index("wide")
    n = lax.axis_index("narrow")
    src_n = lax.div(w, 2)
    base = lax.rem(w + n, N_NARROW)

    def dens_copy(k):
        i, j = k // 4, k % 4
        return pltpu.make_async_copy(
            dens_hbm.at[:, pl.ds(i * BF, BF), pl.ds(j * 128, 128)], dens.at[i, j], dens_sem.at[k]
        )

    for k in range(16):
        dens_copy(k).start()
    info[...] = build_info(blocks, live)

    barrier = pltpu.get_barrier_semaphore()

    for k in range(1, N_WIDE):
        pl.semaphore_signal(barrier, inc=1, device_id=(lax.rem(w + k, N_WIDE), n), device_id_type=MESH)
    for k in range(N_WIDE):

        @pl.when(jnp.logical_or(k != w, src_n != n))
        def _():
            pl.semaphore_signal(barrier, inc=1, device_id=(k, src_n), device_id_type=MESH)

    def coef_copy(t):
        return pltpu.make_async_copy(coef_hbm.at[t], coef.at[t], coef_sem.at[t])

    for t in range(SLOTS):
        coef_copy(t).start()

    @pl.when(src_n == n)
    def _():
        pl.semaphore_wait(barrier, 2 * N_WIDE - 2)

    @pl.when(src_n != n)
    def _():
        pl.semaphore_wait(barrier, 2 * N_WIDE - 1)

    def code_copy(k):
        peer = lax.rem(w + k, N_WIDE)
        return pltpu.make_async_remote_copy(
            src_ref=info, dst_ref=codes.at[w], send_sem=code_send, recv_sem=code_recv,
            device_id=(peer, n), device_id_type=MESH,
        )

    for k in range(1, N_WIDE):
        code_copy(k).start()
    codes[w] = info[...]

    plan[...] = build_plan(blocks, info[...], 2 * base)
    own_copy = pltpu.make_async_copy(plan, own, small_sem.at[0])
    own_copy.start()

    i, k = iota((256, 256), 0), iota((256, 256), 1)
    perm[...] = one_hot(k == (i % 4) * BF + i // 4)

    most = pl.ds(0, N_WIDE - 1)
    pltpu.make_async_copy(codes.at[most], codes.at[most], code_recv).wait()
    codes_copy = pltpu.make_async_copy(codes.at[:, pl.ds(0, 1), :], codes_sm, small_sem.at[1])
    codes_copy.start()
    for k in range(16):
        dens_copy(k).wait()
    own_copy.wait()
    codes_copy.wait()

    def block_copy(k):
        peer = lax.rem(w + k, N_WIDE)
        return pltpu.make_async_remote_copy(
            src_ref=dsend.at[k], dst_ref=dblk.at[w], send_sem=d_send, recv_sem=d_recv,
            device_id=(peer, n), device_id_type=MESH,
        )

    for k in range(1, N_WIDE, 5):
        for j in range(k, k + 5):
            dsend[j] = pack_block(dens, codes_sm[lax.rem(w + j, N_WIDE), 0, w])
        for j in range(k, k + 5):
            block_copy(j).start()
    dblk[w] = pack_block(dens, codes_sm[w, 0, w])
    for t in range(SLOTS):
        coef_copy(t).wait()
    pltpu.make_async_copy(dblk.at[most], dblk.at[most], d_recv).wait()

    def term_copy(i, a, q):
        return pltpu.make_async_remote_copy(
            src_ref=slots[i].at[q], dst_ref=recvs[i].at[w],
            send_sem=t_send.at[i, a], recv_sem=t_recv.at[i],
            device_id=(2 * n + a, q), device_id_type=MESH,
        )

    def is_self(a, q):
        return jnp.logical_and(q == n, 2 * n + a == w)

    def send_terms(i, k):
        m = 4 * PASSES[i][1]
        q = lax.rem(base + k, N_NARROW)
        for b in range(2):
            slots[i][q, b, 0:2 * m] = terms[i][own[1, 2 * q + b]]
            if i == 0:
                slots[i][q, b, 2 * m:2 * m + 16] = label(own[0, 2 * q + b])
        for a in range(2):

            @pl.when(is_self(a, q))
            def _():
                pltpu.make_async_copy(slots[i].at[q], recvs[i].at[w], t_recv.at[i]).start()

            @pl.when(jnp.logical_not(is_self(a, q)))
            def _():
                term_copy(i, a, q).start()

    def run_pass(i):
        start, groups = PASSES[i]

        def task(k, carry):
            t = own[2, k]
            if i == 0:
                spread_block(dblk[own[3, k]], perm, dz.at[k])
            first_step(coef, t, dz.at[k], half, start, groups)

            def finish():
                terms[i][k] = second_step(coef, t, half, groups)

            if groups > 4:
                finish()
            else:
                pl.when(k >= 0)(finish)

            @pl.when(lax.rem(k, 2) == 1)
            def _():
                send_terms(i, lax.div(k, 2))
            return carry

        lax.fori_loop(0, SLOTS, task, 0)

        def rest(k, carry):
            send_terms(i, k)
            return carry

        lax.fori_loop(SLOTS // 2, N_NARROW, rest, 0)

    for i in range(count):
        run_pass(i)

    def wait_sent(i):
        for a in range(2):

            @pl.when(2 * n + a == w)
            def _():
                some = slots[i].at[pl.ds(0, N_NARROW - 1)]
                pltpu.make_async_copy(some, some, t_send.at[i, a]).wait()

            @pl.when(2 * n + a != w)
            def _():
                pltpu.make_async_copy(slots[i], slots[i], t_send.at[i, a]).wait()

    pltpu.make_async_copy(codes.at[most], codes.at[most], code_send).wait()
    pltpu.make_async_copy(dblk.at[most], dblk.at[most], d_send).wait()
    for i in range(count):
        pltpu.make_async_copy(recvs[i], recvs[i], t_recv.at[i]).wait()
        if i == 0:
            m = 4 * PASSES[0][1]
            label_copy = pltpu.make_async_copy(recvs[0].at[:, :, pl.ds(2 * m, 16), :], labels, small_sem.at[0])
            label_copy.start()
            label_copy.wait()
            found[...] = labels[:, :, 0:8, :].astype(F32).astype(jnp.int32)
            table_copy = pltpu.make_async_copy(found.at[:, :, pl.ds(0, 1), :], table, small_sem.at[1])
            table_copy.start()
            table_copy.wait()
        wait_sent(i)


def scatter_kernel(table_hbm, *refs):
    count = len(PASSES)
    recv_hbm, out, recv, (table, sem) = refs[:count], refs[count], refs[count + 1:2 * count + 1], refs[2 * count + 1:]
    wide = lax.axis_index("wide")
    copies = [pltpu.make_async_copy(table_hbm, table, sem.at[count])]
    copies += [pltpu.make_async_copy(recv_hbm[i], recv[i], sem.at[i]) for i in range(count)]
    for copy in copies:
        copy.start()
    out[...] = jnp.zeros_like(out)
    for copy in copies:
        copy.wait()

    def add_slot(k, carry):
        source, b = lax.div(k, 2), lax.rem(k, 2)
        r, c, there = (table[source, b, 0, lane] for lane in range(3))

        @pl.when(jnp.logical_and(there > 0, lax.div(r, 4) == wide))
        def _():
            odd = lax.rem(c, 2)
            rows = lax.rem(r, 4) * BF
            cols = lax.div(lax.rem(c, 8), 2) * 128
            for i in range(count):
                start, m = 4 * PASSES[i][0], 4 * PASSES[i][1]
                keep = iota((2 * m, 128), 1) // BF == odd
                here = recv[i][source, b, 0:2 * m].astype(F32)
                turned = pltpu.roll(here, BF, 1)
                for high in range(2):
                    part = jnp.where(keep, jnp.where(odd == high, here, turned), 0.0)
                    for low in range(2):
                        at = (2 * high + low, pl.ds(rows + start, m), pl.ds(cols, 128))
                        out[at] = out[at] + part[low * m:(low + 1) * m]
        return carry

    lax.fori_loop(0, 2 * N_WIDE, add_slot, 0)


def local(density, coefficients, task_blocks, task_live):
    any_space = pl.BlockSpec(memory_space=pl.ANY)
    smem = pl.BlockSpec(memory_space=pltpu.SMEM)
    dma = pltpu.SemaphoreType.DMA
    count = len(PASSES)
    sizes = [8 * groups for _, groups in PASSES]
    sent = [size + 16 * (i == 0) for i, size in enumerate(sizes)]
    *recv, table = pl.pallas_call(
        exchange_kernel,
        out_shape=[jax.ShapeDtypeStruct((N_WIDE, 2, size, 128), BF16) for size in sent]
        + [jax.ShapeDtypeStruct((N_WIDE, 2, 1, 128), jnp.int32)],
        in_specs=[any_space, any_space, smem, smem],
        out_specs=[any_space] * (count + 1),
        scratch_shapes=[pltpu.VMEM((SLOTS, size, 128), BF16) for size in sizes]
        + [pltpu.VMEM((N_NARROW, 2, size, 128), BF16) for size in sent]
        + [
            pltpu.VMEM((SLOTS, AUXP, BF * BF), BF16),
            pltpu.VMEM((4, 4, NDM, BF, 128), BF16),
            pltpu.VMEM((8, 128), jnp.int32),
            pltpu.VMEM((8, 128), jnp.int32),
            pltpu.SMEM((8, 128), jnp.int32),
            pltpu.VMEM((N_WIDE, 8, 128), jnp.int32),
            pltpu.SMEM((N_WIDE, 1, 128), jnp.int32),
            pltpu.VMEM((N_WIDE, BF, 256), BF16),
            pltpu.VMEM((N_WIDE, BF, 256), BF16),
            pltpu.VMEM((SLOTS, 4, 256, 256), BF16),
            pltpu.VMEM((256, 256), BF16),
            pltpu.VMEM((max(sizes) // 2, 256, AUXP), BF16),
            pltpu.VMEM((N_WIDE, 2, 16, 128), BF16),
            pltpu.VMEM((N_WIDE, 2, 8, 128), jnp.int32),
            dma((SLOTS,)), dma((16,)), dma((2,)),
            dma, dma, dma, dma, dma((count, 2)), dma((count,)),
        ],
        compiler_params=pltpu.CompilerParams(
            collective_id=0, has_side_effects=True, vmem_limit_bytes=56 * 2**20
        ),
        name="exchange",
    )(density, coefficients, task_blocks.T, task_live)
    return pl.pallas_call(
        scatter_kernel,
        out_shape=jax.ShapeDtypeStruct(density.shape, F32),
        in_specs=[any_space] * (count + 1),
        out_specs=pl.BlockSpec(memory_space=pltpu.VMEM),
        scratch_shapes=[pltpu.VMEM((N_WIDE, 2, size, 128), BF16) for size in sent]
        + [
            pltpu.SMEM((N_WIDE, 2, 1, 128), jnp.int32),
            dma((count + 1,)),
        ],
        compiler_params=pltpu.CompilerParams(vmem_limit_bytes=60 * 2**20),
        name="scatter",
    )(table, *recv)


def solution(mesh):
    in_specs = (
        P(None, "wide", "narrow"),
        P(("wide", "narrow"), None, None),
        P(("wide", "narrow"), None),
        P(("wide", "narrow")),
    )
    out_specs = P(None, "wide", "narrow")
    return jax.shard_map(local, mesh=mesh, in_specs=in_specs, out_specs=out_specs, check_vma=False)
```

time: 81.8 us -> 78.5 us (0.960)
  Pallas kernels: 80.6 us -> 76.8 us
    pallas_call x1, Pallas kernels: 76 us -> 73.6 us  [local(): pl.pallas_call(exchange_kernel, out_shape=[jax.ShapeDtypeStruct((N_WIDE,...]
    pallas_call x1, Pallas kernels: 4.6 us -> 3.25 us  [local(): pl.pallas_call(scatter_kernel, out_shape=jax.ShapeDtypeStruct(density.sha...]
where the time goes in v3:
time: 78.5 us; the launch traced here: 77.5 us
  Pallas kernels  76.8 us (98%)
    pallas_call x1, Pallas kernels, local(): pl.pallas_call(exchange_kernel, out_shape=[jax.ShapeDtypeStruct((N_WIDE,...  73.6 us
    pallas_call x1, Pallas kernels, local(): pl.pallas_call(scatter_kernel, out_shape=jax.ShapeDtypeStruct(density.sha...  3.25 us

profile of v3, /device:TPU:97, one launch (start us, length us, event | category | flops | bytes accessed | tf_op | source)
XLA Modules:
  0.0 77.5 jit_solution(6504910044930861892)
XLA Ops:
  0.7 73.6 %exchange.1 = (bf16[16,2,96,128]{3,2,1,0:T(8,128)(2,1)}, bf16[16,2,48,128]{3,2,1,0:T(8,128)(2,1)}, s32[16,2,1,128]{3,2,1,0:T(1,128)}) custom-call(bf16[4,256,512]{2,1,0:T(8,128)(2,1)} %dens_hbm.1, bf16[8,256,4096]{2,1,0:T(8,128)(2,1)} %coef_hbm.1, s32[2,8]{1,0:T(2,128)} %bitcast.1, s32[1]{0:T(128)S(6)} %copy.5.live), custom_call_target="tpu_custom_call" | custom-call | tf_op jit(solution)/shard_map/exchange/pallas_call | solution.py:340
  74.3 3.3 %scatter.1 = f32[4,256,512]{2,1,0:T(8,128)} custom-call(s32[16,2,1,128]{3,2,1,0:T(1,128)} %get-tuple-element.8.table_hbm, bf16[16,2,96,128]{3,2,1,0:T(8,128)(2,1)} %get-tuple-element.9.refs_0_, bf16[16,2,48,128]{3,2,1,0:T(8,128)(2,1)} %get-tuple-element.10.refs_1_), custom_call_target="tpu_custom_call" | custom-call | tf_op jit(solution)/shard_map/scatter/pallas_call | solution.py:371

commit v4 on v3

--- a/solution.py
+++ b/solution.py
@@ -47,7 +47,7 @@
         place = sum((keys[u] < keys[t]).astype(jnp.int32) for u in range(SLOTS) if u != t)
         plan = jnp.where((row == 1) & (lane == stripes[t]), place, plan)
         plan = jnp.where((row == 2) & (lane == place), t, plan)
-        plan = jnp.where((row == 3) & (lane == place), stripes[t], plan)
+        plan = jnp.where((row == 3) & (lane == place), keys[t], plan)
     return plan
 
 
@@ -126,7 +126,7 @@
     w = lax.axis_index("wide")
     n = lax.axis_index("narrow")
     src_n = lax.div(w, 2)
-    base = lax.rem(w + n, N_NARROW)
+    base = lax.div(w, 2)
 
     def dens_copy(k):
         i, j = k // 4, k % 4
@@ -189,22 +189,45 @@
     own_copy.wait()
     codes_copy.wait()
 
+    def peer_of(k):
+        return 2 * lax.rem(base - k // 2 + N_NARROW, N_NARROW) + k % 2
+
     def block_copy(k):
-        peer = lax.rem(w + k, N_WIDE)
         return pltpu.make_async_remote_copy(
-            src_ref=dsend.at[k], dst_ref=dblk.at[w], send_sem=d_send, recv_sem=d_recv,
-            device_id=(peer, n), device_id_type=MESH,
+            src_ref=dsend.at[k], dst_ref=dblk.at[w - 2 * base + k // 2 * 2], send_sem=d_send,
+            recv_sem=d_recv.at[w - 2 * base + k // 2 * 2], device_id=(peer_of(k), n), device_id_type=MESH,
         )
 
-    for k in range(1, N_WIDE, 5):
-        for j in range(k, k + 5):
-            dsend[j] = pack_block(dens, codes_sm[lax.rem(w + j, N_WIDE), 0, w])
-        for j in range(k, k + 5):
-            block_copy(j).start()
-    dblk[w] = pack_block(dens, codes_sm[w, 0, w])
+    near = SLOTS + 2
+    for k in range(0, near, 2):
+        for j in (k, k + 1):
+            dsend[j] = pack_block(dens, codes_sm[peer_of(j), 0, w])
+        for j in (k, k + 1):
+            if j > 1:
+                block_copy(j).start()
+                continue
+
+            @pl.when(peer_of(j) == w)
+            def _():
+                dblk[w - 2 * base] = dsend[j]
+
+            @pl.when(peer_of(j) != w)
+            def _():
+                block_copy(j).start()
+
+    for k in range(near, N_WIDE):
+        dsend[k] = pack_block(dens, codes_sm[peer_of(k), 0, w])
+
+    def wait_block(j):
+        pltpu.make_async_copy(dblk.at[j], dblk.at[j], d_recv.at[j]).wait()
+
+    wait_block(1 - (w - 2 * base))
+    for j in range(2, SLOTS + 1):
+        wait_block(j)
+    for k in range(near, N_WIDE):
+        block_copy(k).start()
     for t in range(SLOTS):
         coef_copy(t).wait()
-    pltpu.make_async_copy(dblk.at[most], dblk.at[most], d_recv).wait()
 
     def term_copy(i, a, q):
         return pltpu.make_async_remote_copy(
@@ -216,13 +239,16 @@
     def is_self(a, q):
         return jnp.logical_and(q == n, 2 * n + a == w)
 
-    def send_terms(i, k):
+    def fill_slots(i, k):
         m = 4 * PASSES[i][1]
         q = lax.rem(base + k, N_NARROW)
         for b in range(2):
             slots[i][q, b, 0:2 * m] = terms[i][own[1, 2 * q + b]]
             if i == 0:
                 slots[i][q, b, 2 * m:2 * m + 16] = label(own[0, 2 * q + b])
+
+    def send_slots(i, k):
+        q = lax.rem(base + k, N_NARROW)
         for a in range(2):
 
             @pl.when(is_self(a, q))
@@ -232,6 +258,13 @@
             @pl.when(jnp.logical_not(is_self(a, q)))
             def _():
                 term_copy(i, a, q).start()
+
+    def label_copy():
+        m = 4 * PASSES[0][1]
+        return pltpu.make_async_copy(recvs[0].at[:, :, pl.ds(2 * m, 16), :], labels, small_sem.at[0])
+
+    def table_copy():
+        return pltpu.make_async_copy(found.at[:, :, pl.ds(0, 1), :], table, small_sem.at[1])
 
     def run_pass(i):
         start, groups = PASSES[i]
@@ -239,7 +272,15 @@
         def task(k, carry):
             t = own[2, k]
             if i == 0:
-                spread_block(dblk[own[3, k]], perm, dz.at[k])
+                @pl.when(k > 0)
+                def _():
+                    wait_block(SLOTS + k)
+
+                block = dblk[k]
+                away = iota((BF, 256), 0) * 0 + own[3, k]
+                for j in range(1, SLOTS + 1):
+                    block = jnp.where(away == k + j, dblk[k + j], block)
+                spread_block(block, perm, dz.at[k])
             first_step(coef, t, dz.at[k], half, start, groups)
 
             def finish():
@@ -252,16 +293,29 @@
 
             @pl.when(lax.rem(k, 2) == 1)
             def _():
-                send_terms(i, lax.div(k, 2))
+                fill_slots(i, lax.div(k, 2))
+                send_slots(i, lax.div(k, 2))
+
+            if i == 1:
+
+                @pl.when(k == SLOTS - 2)
+                def _():
+                    pltpu.make_async_copy(recvs[0], recvs[0], t_recv.at[0]).wait()
+                    label_copy().start()
+
+                @pl.when(k == SLOTS - 1)
+                def _():
+                    label_copy().wait()
+                    found[...] = labels[:, :, 0:8, :].astype(F32).astype(jnp.int32)
+                    table_copy().start()
             return carry
 
         lax.fori_loop(0, SLOTS, task, 0)
 
-        def rest(k, carry):
-            send_terms(i, k)
-            return carry
-
-        lax.fori_loop(SLOTS // 2, N_NARROW, rest, 0)
+        for k in range(SLOTS // 2, N_NARROW):
+            fill_slots(i, k)
+        for k in range(SLOTS // 2, N_NARROW):
+            send_slots(i, k)
 
     for i in range(count):
         run_pass(i)
@@ -280,18 +334,10 @@
 
     pltpu.make_async_copy(codes.at[most], codes.at[most], code_send).wait()
     pltpu.make_async_copy(dblk.at[most], dblk.at[most], d_send).wait()
-    for i in range(count):
-        pltpu.make_async_copy(recvs[i], recvs[i], t_recv.at[i]).wait()
-        if i == 0:
-            m = 4 * PASSES[0][1]
-            label_copy = pltpu.make_async_copy(recvs[0].at[:, :, pl.ds(2 * m, 16), :], labels, small_sem.at[0])
-            label_copy.start()
-            label_copy.wait()
-            found[...] = labels[:, :, 0:8, :].astype(F32).astype(jnp.int32)
-            table_copy = pltpu.make_async_copy(found.at[:, :, pl.ds(0, 1), :], table, small_sem.at[1])
-            table_copy.start()
-            table_copy.wait()
-        wait_sent(i)
+    wait_sent(0)
+    table_copy().wait()
+    pltpu.make_async_copy(recvs[1], recvs[1], t_recv.at[1]).wait()
+    wait_sent(1)
 
 
 def scatter_kernel(table_hbm, *refs):
@@ -361,7 +407,7 @@
             pltpu.VMEM((N_WIDE, 2, 16, 128), BF16),
             pltpu.VMEM((N_WIDE, 2, 8, 128), jnp.int32),
             dma((SLOTS,)), dma((16,)), dma((2,)),
-            dma, dma, dma, dma, dma((count, 2)), dma((count,)),
+            dma, dma, dma, dma((N_WIDE,)), dma((count, 2)), dma((count,)),
         ],
         compiler_params=pltpu.CompilerParams(
             collective_id=0, has_side_effects=True, vmem_limit_bytes=56 * 2**20

time: 78.5 us -> 77.7 us (0.990); the launches traced: 77.5 us -> 77.5 us
  no operation moved by 1% of the time
where the time goes in v4:
time: 77.7 us; the launch traced here: 77.5 us
  Pallas kernels  76.9 us (99%)
    pallas_call x1, Pallas kernels, local(): pl.pallas_call(exchange_kernel, out_shape=[jax.ShapeDtypeStruct((N_WIDE,...  73.3 us
    pallas_call x1, Pallas kernels, local(): pl.pallas_call(scatter_kernel, out_shape=jax.ShapeDtypeStruct(density.sha...  3.5 us

profile of v4, /device:TPU:97, one launch (start us, length us, event | category | flops | bytes accessed | tf_op | source)
XLA Modules:
  0.0 77.5 jit_solution(10994538971886269849)
XLA Ops:
  0.7 73.3 %exchange.1 = (bf16[16,2,96,128]{3,2,1,0:T(8,128)(2,1)}, bf16[16,2,48,128]{3,2,1,0:T(8,128)(2,1)}, s32[16,2,1,128]{3,2,1,0:T(1,128)}) custom-call(bf16[4,256,512]{2,1,0:T(8,128)(2,1)} %dens_hbm.1, bf16[8,256,4096]{2,1,0:T(8,128)(2,1)} %coef_hbm.1, s32[2,8]{1,0:T(2,128)} %bitcast.1, s32[1]{0:T(128)S(6)} %copy.5.live), custom_call_target="tpu_custom_call" | custom-call | tf_op jit(solution)/shard_map/exchange/pallas_call | solution.py:386
  74.0 3.5 %scatter.1 = f32[4,256,512]{2,1,0:T(8,128)} custom-call(s32[16,2,1,128]{3,2,1,0:T(1,128)} %get-tuple-element.8.table_hbm, bf16[16,2,96,128]{3,2,1,0:T(8,128)(2,1)} %get-tuple-element.9.refs_0_, bf16[16,2,48,128]{3,2,1,0:T(8,128)(2,1)} %get-tuple-element.10.refs_1_), custom_call_target="tpu_custom_call" | custom-call | tf_op jit(solution)/shard_map/scatter/pallas_call | solution.py:417

commit v5 on v4

--- a/solution.py
+++ b/solution.py
@@ -1,3 +1,5 @@
+import functools
+
 import jax
 import jax.numpy as jnp
 from jax import lax
@@ -342,7 +344,8 @@
 
 def scatter_kernel(table_hbm, *refs):
     count = len(PASSES)
-    recv_hbm, out, recv, (table, sem) = refs[:count], refs[count], refs[count + 1:2 * count + 1], refs[2 * count + 1:]
+    recv_hbm, out_hbm, recv = refs[:count], refs[count], refs[count + 1:2 * count + 1]
+    out, table, sem = refs[2 * count + 1:]
     wide = lax.axis_index("wide")
     copies = [pltpu.make_async_copy(table_hbm, table, sem.at[count])]
     copies += [pltpu.make_async_copy(recv_hbm[i], recv[i], sem.at[i]) for i in range(count)]
@@ -352,7 +355,7 @@
     for copy in copies:
         copy.wait()
 
-    def add_slot(k, carry):
+    def add_slot(k, carry, high):
         source, b = lax.div(k, 2), lax.rem(k, 2)
         r, c, there = (table[source, b, 0, lane] for lane in range(3))
 
@@ -366,14 +369,20 @@
                 keep = iota((2 * m, 128), 1) // BF == odd
                 here = recv[i][source, b, 0:2 * m].astype(F32)
                 turned = pltpu.roll(here, BF, 1)
-                for high in range(2):
-                    part = jnp.where(keep, jnp.where(odd == high, here, turned), 0.0)
-                    for low in range(2):
-                        at = (2 * high + low, pl.ds(rows + start, m), pl.ds(cols, 128))
-                        out[at] = out[at] + part[low * m:(low + 1) * m]
+                part = jnp.where(keep, jnp.where(odd == high, here, turned), 0.0)
+                for low in range(2):
+                    at = (2 * high + low, pl.ds(rows + start, m), pl.ds(cols, 128))
+                    out[at] = out[at] + part[low * m:(low + 1) * m]
         return carry
 
-    lax.fori_loop(0, 2 * N_WIDE, add_slot, 0)
+    done = []
+    for high in range(2):
+        lax.fori_loop(0, 2 * N_WIDE, functools.partial(add_slot, high=high), 0)
+        pair = pl.ds(2 * high, 2)
+        done.append(pltpu.make_async_copy(out.at[pair], out_hbm.at[pair], sem.at[count + 1 + high]))
+        done[-1].start()
+    for copy in done:
+        copy.wait()
 
 
 def local(density, coefficients, task_blocks, task_live):
@@ -418,11 +427,12 @@
         scatter_kernel,
         out_shape=jax.ShapeDtypeStruct(density.shape, F32),
         in_specs=[any_space] * (count + 1),
-        out_specs=pl.BlockSpec(memory_space=pltpu.VMEM),
+        out_specs=any_space,
         scratch_shapes=[pltpu.VMEM((N_WIDE, 2, size, 128), BF16) for size in sent]
         + [
+            pltpu.VMEM(density.shape, F32),
             pltpu.SMEM((N_WIDE, 2, 1, 128), jnp.int32),
-            dma((count + 1,)),
+            dma((count + 3,)),
         ],
         compiler_params=pltpu.CompilerParams(vmem_limit_bytes=60 * 2**20),
         name="scatter",

time: 77.7 us -> 78.3 us (level)
  no operation moved by 1% of the time
where the time goes in v5:
time: 78.3 us
  Pallas kernels  77.6 us (99%)
    pallas_call x1, Pallas kernels, local(): pl.pallas_call(exchange_kernel, out_shape=[jax.ShapeDtypeStruct((N_WIDE,...  73.3 us
    pallas_call x1, Pallas kernels, local(): pl.pallas_call(scatter_kernel, out_shape=jax.ShapeDtypeStruct(density.sha...  4.25 us

profile of v5, /device:TPU:97, one launch (start us, length us, event | category | flops | bytes accessed | tf_op | source)
XLA Modules:
  0.0 78.3 jit_solution(17961056725008302305)
XLA Ops:
  0.7 73.3 %exchange.1 = (bf16[16,2,96,128]{3,2,1,0:T(8,128)(2,1)}, bf16[16,2,48,128]{3,2,1,0:T(8,128)(2,1)}, s32[16,2,1,128]{3,2,1,0:T(1,128)}) custom-call(bf16[4,256,512]{2,1,0:T(8,128)(2,1)} %dens_hbm.1, bf16[8,256,4096]{2,1,0:T(8,128)(2,1)} %coef_hbm.1, s32[2,8]{1,0:T(2,128)} %bitcast.1, s32[1]{0:T(128)S(6)} %copy.5.live), custom_call_target="tpu_custom_call" | custom-call | tf_op jit(solution)/shard_map/exchange/pallas_call | solution.py:395
  74.0 4.2 %scatter.1 = f32[4,256,512]{2,1,0:T(8,128)} custom-call(s32[16,2,1,128]{3,2,1,0:T(1,128)} %get-tuple-element.8.table_hbm, bf16[16,2,96,128]{3,2,1,0:T(8,128)(2,1)} %get-tuple-element.9.refs_0_, bf16[16,2,48,128]{3,2,1,0:T(8,128)(2,1)} %get-tuple-element.10.refs_1_), custom_call_target="tpu_custom_call" | custom-call | tf_op jit(solution)/shard_map/scatter/pallas_call | solution.py:426
